TPU v7x, 256 devices: a whole 4x4x8 slice. The times are simulated.
256 devices in a mesh: dp: 8 (over x, core), expert: 32 (over y, z).
Axes of the slice: x: 4, y: 4, z: 8, core: 2. Of those that a mesh axis runs over, the one named last changes fastest.
Arguments:
- tokens: bfloat16 [32768, 3072], P(('dp', 'expert')), may hold values from -6 to 6
- routes: int32 [32768, 2], P(('dp', 'expert')), may hold values from 0 to 31, as said below
- router_gates: int32 [32768, 2], P(('dp', 'expert')), may hold values from 1024 to 32767
- hidden_cotangent: bfloat16 [32768, 2, 768], P(('dp', 'expert')), may hold values from -6 to 6
- weights: bfloat16 [2, 32, 768, 3072], P(None, None, 'expert', 'dp'), may hold values from -0.109375 to 0.109375
- first_moment: bfloat16 [2, 32, 768, 3072], P(None, None, 'expert', 'dp'), may hold values from -6 to 6
- second_moment: bfloat16 [2, 32, 768, 3072], P(None, None, 'expert', 'dp'), may hold values from 0.5 to 4
Outputs:
- token_grads: bfloat16 [32768, 3072], P(('dp', 'expert'))
- new_weights: bfloat16 [2, 32, 768, 3072], P(None, 'expert', None, 'dp')
- new_first: bfloat16 [2, 32, 768, 3072], P(None, 'expert', None, 'dp')
- new_second: bfloat16 [2, 32, 768, 3072], P(None, 'expert', None, 'dp')
Inputs may be any that keep to these rules, and one draw needn't show every extreme that they name: `routes`: each row names 2 different experts; the rows of one device name any one expert at most 12 times.
All inputs are finite; a program needn't handle non-finite values.
Results may differ from a plain program's by a relative error of at most 0.0075.
Values may be sent and summed in bfloat16 or wider, within the bound.
A program may use at most 128 MiB of HBM per device.

v0:
```python
import jax
import jax.numpy as jnp
from jax import lax
from jax.sharding import PartitionSpec as P

gate_unit = 32768.0
loss_scale = 16.0
beta_one = 0.9
beta_two = 0.95
step_size = 0.001
adam_eps = 1e-08


def per_device(
    tokens, routes, router_gates, hidden_cotangent, weights, first_moment, second_moment
):
    row_count = tokens.shape[0]
    model_width = tokens.shape[1]
    per_token = routes.shape[1]
    hidden_units = hidden_cotangent.shape[2]
    experts = weights.shape[1]
    capacity = 3 * row_count * per_token // (2 * experts)
    routings = row_count * per_token
    owned_weights, owned_first, owned_second = (
        lax.all_to_all(weights, "expert", split_axis=1, concat_axis=2, tiled=True),
        lax.all_to_all(first_moment, "expert", split_axis=1, concat_axis=2, tiled=True),
        lax.all_to_all(second_moment, "expert", split_axis=1, concat_axis=2, tiled=True),
    )
    full_weights = lax.all_gather(owned_weights, "dp", axis=3, tiled=True)[:, 0]
    flat_route = routes.reshape(-1)
    onehot = (flat_route[:, None] == jnp.arange(experts, dtype=jnp.int32)[None, :]).astype(
        jnp.int32
    )
    position = jnp.sum((jnp.cumsum(onehot, axis=0) - onehot) * onehot, axis=1)
    target = flat_route * capacity + position
    routing_ids = jnp.arange(routings, dtype=jnp.int32)
    slot_table = jnp.full((experts * capacity,), routings, jnp.int32).at[target].set(routing_ids)
    filled = slot_table < routings
    token_index = jnp.where(filled, slot_table // per_token, 0)
    gate_factor = router_gates.astype(jnp.float32) / gate_unit
    scaled = (gate_factor[:, :, None] * hidden_cotangent.astype(jnp.float32)).astype(jnp.bfloat16)
    scaled = scaled.reshape(routings, hidden_units)
    send_rows = jnp.where(
        filled[:, None], jnp.take(tokens, token_index, axis=0), jnp.zeros((), jnp.bfloat16)
    )
    send_rows = send_rows.reshape(experts, capacity, model_width)
    send_grads = jnp.where(
        filled[:, None],
        jnp.take(scaled, jnp.minimum(slot_table, routings - 1), axis=0),
        jnp.zeros((), jnp.bfloat16),
    )
    send_grads = send_grads.reshape(experts, capacity, hidden_units)
    rows_in = lax.all_to_all(send_rows, "expert", split_axis=0, concat_axis=0, tiled=True)
    grads_in = lax.all_to_all(send_grads, "expert", split_axis=0, concat_axis=0, tiled=True)
    sources = rows_in.shape[0]
    slots_in = rows_in.shape[1]
    flat_rows = rows_in.reshape(sources * slots_in, model_width)
    projected = jnp.einsum(
        "rd,ahd->rah", flat_rows, full_weights, preferred_element_type=jnp.float32
    )
    pre_gate = projected[:, 0]
    pre_up = projected[:, 1]
    sigmoid_gate = jax.nn.sigmoid(pre_gate)
    upstream = grads_in.reshape(sources * slots_in, hidden_units).astype(jnp.float32)
    grad_up = (upstream * pre_gate * sigmoid_gate).astype(jnp.bfloat16)
    grad_gate = (upstream * pre_up * sigmoid_gate * (1.0 + pre_gate * (1.0 - sigmoid_gate))).astype(
        jnp.bfloat16
    )
    paired = jnp.stack([grad_gate, grad_up], axis=1)
    backward = jnp.einsum(
        "rah,ahd->rd", paired, full_weights, preferred_element_type=jnp.float32
    ).astype(jnp.bfloat16)
    backward, paired, received = (
        backward.reshape(sources, slots_in, model_width),
        paired.reshape(sources, slots_in, 2, hidden_units),
        rows_in,
    )
    returned = lax.all_to_all(backward, "expert", split_axis=0, concat_axis=0, tiled=True)
    selector = (token_index[None, :] == jnp.arange(row_count, dtype=jnp.int32)[:, None]) & filled[
        None, :
    ]
    token_grads = jnp.dot(
        selector.astype(jnp.bfloat16),
        returned.reshape(experts * capacity, model_width),
        preferred_element_type=jnp.float32,
    ).astype(jnp.bfloat16)
    received_count = received.shape[0] * received.shape[1]
    rows_mat = received.reshape(received_count, model_width)
    paired_mat = paired.reshape(received_count, 2, hidden_units)
    partial_sum = jnp.einsum(
        "rah,rd->ahd", paired_mat, rows_mat, preferred_element_type=jnp.float32
    )
    summed = lax.psum_scatter(
        partial_sum.astype(jnp.bfloat16), "dp", scatter_dimension=2, tiled=True
    ).astype(jnp.float32)
    gradient = (summed / loss_scale)[:, None]
    moment_one = beta_one * owned_first.astype(jnp.float32) + (1.0 - beta_one) * gradient
    moment_two = (
        beta_two * owned_second.astype(jnp.float32) + (1.0 - beta_two) * gradient * gradient
    )
    updated = owned_weights.astype(jnp.float32) - step_size * moment_one / (
        jnp.sqrt(moment_two) + adam_eps
    )
    return (
        token_grads,
        updated.astype(jnp.bfloat16),
        moment_one.astype(jnp.bfloat16),
        moment_two.astype(jnp.bfloat16),
    )


def solution(mesh):
    placed = (
        P(("dp", "expert"), None),
        P(("dp", "expert"), None),
        P(("dp", "expert"), None),
        P(("dp", "expert"), None, None),
        P(None, None, "expert", "dp"),
        P(None, None, "expert", "dp"),
        P(None, None, "expert", "dp"),
    )
    return jax.shard_map(
        per_device,
        mesh=mesh,
        in_specs=placed,
        out_specs=(
            P(("dp", "expert"), None),
            P(None, "expert", None, "dp"),
            P(None, "expert", None, "dp"),
            P(None, "expert", None, "dp"),
        ),
        check_vma=False,
    )
```

profile of v0, /device:TPU:6, one launch (start us, length us, event | category | flops | bytes accessed | tf_op | source)
XLA Modules:
  0.0 397.2 jit_solution(6819579921525922149)
XLA Ops:
  7.2 1.5 copy.44
  8.7 44.2 %all_to_all.45 = bf16[2,32,24,384]{3,2,0,1:T(8,128)(2,1)S(1)} all-to-all(bf16[2,32,24,384]{3,2,0,1:T(8,128)(2,1)S(1)} %copy.44), channel_id=1, replica_groups=mesh['dp'=8,'expert'=32] {'expert'}, dimensions={1} | all-to-all | bytes 2359296 | tf_op jit(solution)/shard_map/all_to_all | solution.py:25
  52.9 1.1 copy.45
  54.3 0.1 eq.42
  54.6 0.4 multiply_convert_fusion.1
  55.0 0.1 reshape.157
  55.3 0.1 mul.98
  55.5 0.6 reduce-window.6
  56.0 0.2 slice_reduce_fusion
  56.4 1.4 scatter_custom_fusion
  57.8 2.2 gather_fusion
  60.4 1.1 select_select_fusion.1
  61.5 4.6 %all-to-all-start = ((bf16[32,12,768]{2,1,0:T(8,128)(2,1)}), bf16[32,12,768]{2,1,0:T(8,128)(2,1)}, u32[]{:S(2)}, u32[]{:S(2)}) async-start(bf16[32,12,768]{2,1,0:T(8,128)(2,1)} %select_select_fusion.1), calls=%async_computation | async-start | bytes 1572864 | tf_op jit(solution)/shard_map/all_to_all | solution.py:54
  66.2 2.9 gather_fusion.1
  69.1 2.4 gather.15
  71.6 4.0 %select_select_fusion = bf16[32,12,3072]{2,1,0:T(8,128)(2,1)} fusion(bf16[32,12,3072]{2,1,0:T(8,128)(2,1)} %gather.15, pred[32,12]{1,0:T(8,128)(4,1)S(1)} %broadcast_in_dim.73, pred[32,12]{1,0:T(8,128)(4,1)S(1)} %broadcast_in_dim.65), kind=kLoop, calls=%fused_computation.13 | loop fusion | flops 2359296 | bytes 4719360 | tf_op jit(solution)/shard_map/jit(_where)/select_n | solution.py:43
  75.6 12.5 %all-to-all-done = bf16[32,12,768]{2,1,0:T(8,128)(2,1)} async-done(((bf16[32,12,768]{2,1,0:T(8,128)(2,1)}), bf16[32,12,768]{2,1,0:T(8,128)(2,1)}, u32[]{:S(2)}, u32[]{:S(2)}) %all-to-all-start) | async-done | bytes 589856 | tf_op jit(solution)/shard_map/all_to_all | solution.py:54
  88.1 5.1 %all-to-all-start.1 = ((bf16[32,12,3072]{2,1,0:T(8,128)(2,1)}), bf16[32,12,3072]{2,1,0:T(8,128)(2,1)}, u32[]{:S(2)}, u32[]{:S(2)}) async-start(bf16[32,12,3072]{2,1,0:T(8,128)(2,1)} %select_select_fusion), calls=%async_computation.1 | async-start | bytes 6291456 | tf_op jit(solution)/shard_map/all_to_all | solution.py:53
  93.2 0.2 reduce-scatter.4.cloned.1.call-start
  93.4 1.3 reshape.161
  94.7 72.0 %all-to-all-done.1 = bf16[32,12,3072]{2,1,0:T(8,128)(2,1)} async-done(((bf16[32,12,3072]{2,1,0:T(8,128)(2,1)}), bf16[32,12,3072]{2,1,0:T(8,128)(2,1)}, u32[]{:S(2)}, u32[]{:S(2)}) %all-to-all-start.1) | async-done | bytes 2359328 | tf_op jit(solution)/shard_map/all_to_all | solution.py:53
  166.7 4.3 %reshape.189 = bf16[384,3072,1]{1,0,2:T(8,128)(2,1)} reshape(bf16[32,12,3072]{2,1,0:T(8,128)(2,1)} %all-to-all-done.1) | data formatting | bytes 4718592 | tf_op jit(solution)/shard_map/reshape | solution.py:57
  171.0 7.2 %fusion.2 = f32[384,2,768]{2,0,1:T(8,128)S(1)} fusion(bf16[384,3072,1]{1,0,2:T(8,128)(2,1)} %reshape.189, bf16[2,1,768,3072]{3,2,0,1:T(8,128)(2,1)} %all-gather.2.cloned.1.call-done), kind=kOutput, calls=%fused_computation.5 | convolution fusion | flops 3623878656 | bytes 14155776 | tf_op jit(solution)/shard_map/rd,ahd->rah/dot_general | solution.py:58
  178.2 0.7 fusion.14
  178.9 0.8 copy-done.6
  179.7 0.1 copy-done.3
  179.9 7.7 %convolution_convert_fusion = bf16[2,768,3072]{2,1,0:T(8,128)(2,1)} fusion(bf16[384,3072,1]{1,0,2:T(8,128)(2,1)S(1)} %copy-done.3, bf16[384,1,768]{2,0,1:T(8,128)(2,1)S(1)} %get-tuple-element.26, bf16[384,1,768]{2,0,1:T(8,128)(2,1)S(1)} %get-tuple-element.25), kind=kOutput, calls=%fused_computation.7 | convolution fusion | flops 3629187072 | bytes 12976128 | tf_op jit(solution)/shard_map/rah,rd->ahd/dot_general | solution.py:90
  187.6 23.8 %copy.56 = bf16[2,768,3072]{1,0,2:T(2,128)(2,1)} copy(bf16[2,768,3072]{2,1,0:T(8,128)(2,1)} %convolution_convert_fusion) | data formatting | bytes 18874368
  211.3 9.0 %copy.59 = bf16[384,8,2,768]{3,1,2,0:T(8,128)(2,1)} copy(bf16[384,8,2,768]{3,2,1,0:T(2,128)(2,1)} %bitcast.63) | data formatting | bytes 18874368
  220.4 1.2 copy-done.4
  221.6 1.1 copy.50
  222.8 4.0 %all-to-all-start.5 = ((bf16[2,32,24,384]{3,2,0,1:T(8,128)(2,1)}), bf16[2,32,24,384]{3,2,0,1:T(8,128)(2,1)S(1)}, u32[]{:S(2)}, u32[]{:S(2)}) async-start(bf16[2,32,24,384]{3,2,0,1:T(8,128)(2,1)} %copy.50), calls=%async_computation.5 | async-start | bytes 2359296 | tf_op jit(solution)/shard_map/all_to_all | solution.py:27
  226.8 1.1 copy.47
  228.0 30.1 %all-to-all-done.5 = bf16[2,32,24,384]{3,2,0,1:T(8,128)(2,1)S(1)} async-done(((bf16[2,32,24,384]{3,2,0,1:T(8,128)(2,1)}), bf16[2,32,24,384]{3,2,0,1:T(8,128)(2,1)S(1)}, u32[]{:S(2)}, u32[]{:S(2)}) %all-to-all-start.5) | async-done | bytes 1179680 | tf_op jit(solution)/shard_map/all_to_all | solution.py:27
  258.1 5.2 %all-to-all-start.4 = ((bf16[2,32,24,384]{3,2,0,1:T(8,128)(2,1)}), bf16[2,32,24,384]{3,2,0,1:T(8,128)(2,1)S(1)}, u32[]{:S(2)}, u32[]{:S(2)}) async-start(bf16[2,32,24,384]{3,2,0,1:T(8,128)(2,1)} %copy.47), calls=%async_computation.4 | async-start | bytes 2359296 | tf_op jit(solution)/shard_map/all_to_all | solution.py:26
  263.2 9.3 %bitcast_convert_fusion = bf16[384,3072]{1,0:T(8,128)(2,1)} fusion(bf16[2,1,768,3072]{3,2,0,1:T(8,128)(2,1)} %all-gather.2.cloned.1.call-done, bf16[384,1,768]{2,0,1:T(8,128)(2,1)} %copy-done.6, bf16[384,1,768]{2,0,1:T(8,128)(2,1)S(1)} %get-tuple-element.25), kind=kOutput, calls=%fused_computation.8 | convolution fusion | flops 3625648128 | bytes 12976128 | tf_op jit(solution)/shard_map/rah,ahd->rd/dot_general | solution.py:70
  272.5 4.2 %reshape.159 = bf16[32,12,3072]{2,1,0:T(8,128)(2,1)} reshape(bf16[384,3072]{1,0:T(8,128)(2,1)} %bitcast_convert_fusion) | data formatting | bytes 4718592 | tf_op jit(solution)/shard_map/reshape | solution.py:74
  276.8 17.5 %all-to-all-done.4 = bf16[2,32,24,384]{3,2,0,1:T(8,128)(2,1)S(1)} async-done(((bf16[2,32,24,384]{3,2,0,1:T(8,128)(2,1)}), bf16[2,32,24,384]{3,2,0,1:T(8,128)(2,1)S(1)}, u32[]{:S(2)}, u32[]{:S(2)}) %all-to-all-start.4) | async-done | bytes 1179680 | tf_op jit(solution)/shard_map/all_to_all | solution.py:26
  294.3 5.3 %all-to-all-start.3 = ((bf16[32,12,3072]{2,1,0:T(8,128)(2,1)}), bf16[32,12,3072]{2,1,0:T(8,128)(2,1)}, u32[]{:S(2)}, u32[]{:S(2)}) async-start(bf16[32,12,3072]{2,1,0:T(8,128)(2,1)} %reshape.159), calls=%async_computation.3 | async-start | bytes 6291456 | tf_op jit(solution)/shard_map/all_to_all | solution.py:78
  299.6 0.2 convert_multiply_fusion.3
  299.8 1.6 copy.51
  301.5 1.6 convert_multiply_fusion.4
  303.1 70.4 %all-to-all-done.3 = bf16[32,12,3072]{2,1,0:T(8,128)(2,1)} async-done(((bf16[32,12,3072]{2,1,0:T(8,128)(2,1)}), bf16[32,12,3072]{2,1,0:T(8,128)(2,1)}, u32[]{:S(2)}, u32[]{:S(2)}) %all-to-all-start.3) | async-done | bytes 2359328 | tf_op jit(solution)/shard_map/all_to_all | solution.py:78
  373.5 2.8 reshape.160
  376.3 1.5 convolution_convert_fusion.1
  377.8 3.0 reshape.193
  380.8 3.2 copy.57
  384.0 6.3 %fusion.11 = (bf16[2,768,384]{2,1,0:T(8,128)(2,1)}, bf16[2,768,384]{2,1,0:T(8,128)(2,1)}, bf16[2,768,384]{2,1,0:T(8,128)(2,1)}) fusion(bf16[2,768,384]{2,1,0:T(8,128)(2,1)} %copy.57, f32[2,32,24,384]{3,2,1,0:T(8,128)} %copy.51, f32[2,32,24,384]{3,2,1,0:T(8,128)} %convert_multiply_fusion.4, bf16[2,32,24,384]{3,2,1,0:T(8,128)(2,1)S(1)} %copy-done.2), kind=kLoop, calls=%fused_computation.22 | loop fusion | flops 8847360 | bytes 10616832 | tf_op jit(solution)/shard_map/convert_element_type | solution.py:108
  (43 shorter events, 1.3 us)
Async XLA Ops:
  7.2 59.0 %copy-start = (bf16[128,3072]{1,0:T(8,128)(2,1)S(1)}, bf16[128,3072]{1,0:T(8,128)(2,1)}, u32[]{:S(2)}) copy-start(bf16[128,3072]{1,0:T(8,128)(2,1)} %param.7) | copy-start | bytes 2359300
  7.2 163.8 %all-gather.2.cloned.1.call-start = ((), (), s32[]{:S(2)}) async-start(), calls=%async_computation.7 | async-start | bytes 10616832 | tf_op jit(solution)/shard_map/all_gather | solution.py:29
  52.9 1.2 copy-start.8
  52.9 1.6 copy-start.9
  52.9 1.7 copy-start.7
  61.5 26.6 %all-to-all-start = ((bf16[32,12,768]{2,1,0:T(8,128)(2,1)}), bf16[32,12,768]{2,1,0:T(8,128)(2,1)}, u32[]{:S(2)}, u32[]{:S(2)}) async-start(bf16[32,12,768]{2,1,0:T(8,128)(2,1)} %select_select_fusion.1), calls=%async_computation | async-start | bytes 1572864 | tf_op jit(solution)/shard_map/all_to_all | solution.py:54
  88.1 78.6 %all-to-all-start.1 = ((bf16[32,12,3072]{2,1,0:T(8,128)(2,1)}), bf16[32,12,3072]{2,1,0:T(8,128)(2,1)}, u32[]{:S(2)}, u32[]{:S(2)}) async-start(bf16[32,12,3072]{2,1,0:T(8,128)(2,1)} %select_select_fusion), calls=%async_computation.1 | async-start | bytes 6291456 | tf_op jit(solution)/shard_map/all_to_all | solution.py:53
  93.2 284.6 %reduce-scatter.4.cloned.1.call-start = ((), (), s32[]{:S(2)}) async-start(), calls=%async_computation.8 | async-start | bytes 10616832
  178.2 1.7 copy-start.3
  178.9 0.8 copy-start.6
  220.4 1.3 copy-start.4
  221.6 5.2 %copy-start.5 = (bf16[2,32,24,384]{3,2,1,0:T(8,128)(2,1)S(1)}, bf16[2,32,24,384]{3,2,1,0:T(8,128)(2,1)}, u32[]{:S(2)}) copy-start(bf16[2,32,24,384]{3,2,1,0:T(8,128)(2,1)} %param.12) | copy-start | bytes 3538948
  222.8 35.3 %all-to-all-start.5 = ((bf16[2,32,24,384]{3,2,0,1:T(8,128)(2,1)}), bf16[2,32,24,384]{3,2,0,1:T(8,128)(2,1)S(1)}, u32[]{:S(2)}, u32[]{:S(2)}) async-start(bf16[2,32,24,384]{3,2,0,1:T(8,128)(2,1)} %copy.50), calls=%async_computation.5 | async-start | bytes 2359296 | tf_op jit(solution)/shard_map/all_to_all | solution.py:27
  258.1 36.2 %all-to-all-start.4 = ((bf16[2,32,24,384]{3,2,0,1:T(8,128)(2,1)}), bf16[2,32,24,384]{3,2,0,1:T(8,128)(2,1)S(1)}, u32[]{:S(2)}, u32[]{:S(2)}) async-start(bf16[2,32,24,384]{3,2,0,1:T(8,128)(2,1)} %copy.47), calls=%async_computation.4 | async-start | bytes 2359296 | tf_op jit(solution)/shard_map/all_to_all | solution.py:26
  294.3 79.2 %all-to-all-start.3 = ((bf16[32,12,3072]{2,1,0:T(8,128)(2,1)}), bf16[32,12,3072]{2,1,0:T(8,128)(2,1)}, u32[]{:S(2)}, u32[]{:S(2)}) async-start(bf16[32,12,3072]{2,1,0:T(8,128)(2,1)} %reshape.159), calls=%async_computation.3 | async-start | bytes 6291456 | tf_op jit(solution)/shard_map/all_to_all | solution.py:78
  377.8 6.2 %copy-start.2 = (bf16[2,32,24,384]{3,2,1,0:T(8,128)(2,1)S(1)}, bf16[2,32,24,384]{3,2,1,0:T(8,128)(2,1)}, u32[]{:S(2)}) copy-start(bf16[2,32,24,384]{3,2,1,0:T(8,128)(2,1)} %copy.45) | copy-start | bytes 3538948
  384.0 6.3 %copy-start.1 = (bf16[128,3072]{1,0:T(8,128)(2,1)S(1)}, bf16[128,3072]{1,0:T(8,128)(2,1)}, u32[]{:S(2)}) copy-start(bf16[128,3072]{1,0:T(8,128)(2,1)} %param.7) | copy-start | bytes 2359300
Sparse Core Ops, SparseCore 0:
  54.2 49.6 all-gather.1
  220.5 53.5 reduce-scatter.3
where the time goes:
time: 399 us; the launch traced here: 397 us
  waiting for transfers between devices  203 us (51%)
  local copies, waits for them, and re-layouts  70.7 us (18%)
  blocking collectives  44.2 us (11%)
  matrix products  25.6 us (6%)
  starting transfers between devices  24.6 us (6%)
  other arithmetic  15.1 us (4%)
  between operations  14.3 us (4%)
    all_to_all x1, waiting for transfers between devices, per_device(): lax.all_to_all(send_rows, 'expert', split_axis=0, concat_axis=0, tiled=True)  72 us
    all_to_all x1, waiting for transfers between devices, per_device(): lax.all_to_all(backward, 'expert', split_axis=0, concat_axis=0, tiled=True)  70.4 us
    unnamed x28, local copies, waits for them, and re-layouts  45.1 us
    all_to_all x1, blocking collectives, per_device(): lax.all_to_all(weights, 'expert', split_axis=1, concat_axis=2, tiled=True)  44.2 us
    all_to_all x1, waiting for transfers between devices, per_device(): lax.all_to_all(second_moment, 'expert', split_axis=1, concat_axis=2, tile...  30.1 us
    all_to_all x1, waiting for transfers between devices, per_device(): lax.all_to_all(first_moment, 'expert', split_axis=1, concat_axis=2, tiled...  17.5 us
    all_to_all x1, waiting for transfers between devices, per_device(): lax.all_to_all(send_grads, 'expert', split_axis=0, concat_axis=0, tiled=T...  12.5 us
    dot_general x1, matrix products, per_device(): jnp.einsum('rah,ahd->rd', paired, full_weights, preferred_element_type=jn...  9.3 us
  transfers between devices with their start and end apart: 7, of which 5 were waited for; matrix products, arithmetic and copies ran while one was open for 12% of the time, Pallas kernels for 0%

commit v1 on v0

v1 whole, which is shorter than its diff:
```python
import functools

import jax
import jax.numpy as jnp
import numpy as np
from jax import lax
from jax.experimental import pallas as pl
from jax.experimental.pallas import tpu as pltpu
from jax.sharding import PartitionSpec as P

gate_unit = 32768.0
loss_scale = 16.0
beta_one = 0.9
beta_two = 0.95
step_size = 0.001
adam_eps = 1e-08

MESH = pl.DeviceIdType.MESH
F32 = jnp.float32
BF16 = jnp.bfloat16
CORES = 2
QUARTERS = 4
HALVES = 2
GROUP = 4
W, ROWS, COTS, M1, M2, BACK = range(6)


def dot(a, b, dims=((1,), (0,))):
    return lax.dot_general(a, b, (dims, ((), ())), preferred_element_type=F32)


def kernel(
    nx,
    ny,
    nz,
    cap,
    routes_row,
    routes_col,
    tokens,
    scaled,
    swap,
    fold,
    w,
    m1,
    m2,
    token_out,
    w_out,
    m1_out,
    m2_out,
    rows_s,
    rows_r,
    cots_s,
    cots_r,
    w_r,
    m1_r,
    m2_r,
    full_w,
    x_mat,
    cot_mat,
    pair,
    pair_t,
    back_r,
    grads,
    half_r,
    quarter_r,
    send,
    recv,
    gather_send,
    gather_recv,
    twin_send,
    twin_recv,
    half_send,
    half_recv,
    sum_send,
    sum_recv,
):
    n = ny * nz
    dp, me = lax.axis_index("dp"), lax.axis_index("expert")
    x, core = dp // CORES, dp % CORES
    y, z = me // nz, me % nz
    twin = x * CORES + 1 - core
    tok, width = tokens.shape
    hidden = scaled.shape[1] // 2
    quarter, half = width // QUARTERS, hidden // HALVES
    per_source, cols = w.shape[2], w.shape[3]
    block = QUARTERS * cap
    cot_block = HALVES * cap
    groups = n // GROUP
    span = GROUP * cap
    slots = n * cap

    def peer(i):
        return lax.rem(y + i // nz, ny) * nz + lax.rem(z + i % nz, nz)

    def x_peer(d):
        return lax.rem(x + d, nx) * CORES + core

    barrier = pltpu.get_barrier_semaphore()

    def greet(i, _):
        pl.semaphore_signal(barrier, inc=1, device_id=(dp, peer(i)), device_id_type=MESH)
        return 0

    lax.fori_loop(1, n, greet, 0)
    for d in range(1, nx):
        pl.semaphore_signal(barrier, inc=1, device_id=(x_peer(d), me), device_id_type=MESH)
    pl.semaphore_signal(barrier, inc=1, device_id=(twin, me), device_id_type=MESH)
    pl.semaphore_wait(barrier, n - 1 + nx - 1 + 1)

    def spread(kind, source, landing):
        def start(i, _):
            to = peer(i)
            pltpu.make_async_remote_copy(
                src_ref=source(to),
                dst_ref=landing(me),
                send_sem=send.at[kind],
                recv_sem=recv.at[kind],
                device_id=(dp, to),
                device_id_type=MESH,
            ).start()
            return 0

        lax.fori_loop(1, n, start, 0)
        pltpu.make_async_copy(source(me), landing(me), recv.at[kind]).start()

    def arrived(kind, ref):
        pltpu.make_async_copy(ref, ref, recv.at[kind]).wait()

    def left(kind, ref):
        pltpu.make_async_copy(ref, ref, send.at[kind]).wait()

    spread(W, lambda e: w.at[:, e], lambda s: w_r.at[:, s])

    experts = n
    earlier = lax.broadcasted_iota(jnp.int32, (tok, tok), 0)
    later = lax.broadcasted_iota(jnp.int32, (tok, tok), 1)
    ids = lax.broadcasted_iota(jnp.int32, (experts, tok), 0)
    route_rows = [routes_row[k : k + 1, :] for k in range(2)]
    hot = [(ids == r).astype(F32) for r in route_rows]
    before = dot((hot[0] + hot[1]).astype(BF16), (earlier < later).astype(BF16))
    pos_row = [jnp.sum(h * before, axis=0, keepdims=True).astype(jnp.int32) for h in hot]

    piece = lax.broadcasted_iota(jnp.int32, (GROUP * block, tok), 0)
    cot_piece = lax.broadcasted_iota(jnp.int32, (GROUP * cot_block, tok), 0)

    def pack(g, _):
        first = g * (GROUP * block)
        total = jnp.zeros((GROUP * block, quarter), F32)
        for q in range(QUARTERS):
            spot = [r * block + p + q * cap - first for r, p in zip(route_rows, pos_row)]
            pick = (piece == spot[0]) | (piece == spot[1])
            total += dot(pick.astype(BF16), tokens[:, q * quarter : (q + 1) * quarter])
        rows_s[pl.ds(g * GROUP, GROUP)] = total.astype(BF16).reshape(GROUP, block, quarter)
        first = g * (GROUP * cot_block)
        total = jnp.zeros((GROUP * cot_block, half), F32)
        for k in range(2):
            for h in range(HALVES):
                spot = route_rows[k] * cot_block + pos_row[k] + h * cap - first
                pick = (cot_piece == spot).astype(BF16)
                start = k * hidden + h * half
                total += dot(pick, scaled[:, start : start + half])
        cots_s[pl.ds(g * GROUP, GROUP)] = total.reshape(GROUP, cot_block, half).astype(BF16)
        return 0

    lax.fori_loop(0, groups, pack, 0)

    left(W, w_r.at[:, pl.ds(0, n - 1)])
    spread(COTS, lambda e: cots_s.at[e], lambda s: cots_r.at[s])
    spread(ROWS, lambda e: rows_s.at[e], lambda s: rows_r.at[s])

    arrived(W, w_r)

    def own_columns(i, _):
        for a in range(2):
            part = w_r[a, pl.ds(i * GROUP, GROUP)].astype(F32)
            rows = GROUP * per_source
            full_w[dp, pl.ds(a * hidden + i * rows, rows), :] = part.reshape(rows, cols).astype(BF16)
        return 0

    lax.fori_loop(0, groups, own_columns, 0)

    def gather(d):
        return pltpu.make_async_remote_copy(
            src_ref=full_w.at[dp],
            dst_ref=full_w.at[dp],
            send_sem=gather_send.at[d - 1],
            recv_sem=gather_recv.at[d - 1],
            device_id=(x_peer(d), me),
            device_id_type=MESH,
        )

    def hand_over(d):
        held = lax.rem(x - d + nx, nx) * CORES + core
        return pltpu.make_async_remote_copy(
            src_ref=full_w.at[held],
            dst_ref=full_w.at[held],
            send_sem=twin_send.at[d],
            recv_sem=twin_recv.at[d],
            device_id=(twin, me),
            device_id_type=MESH,
        )

    for d in range(1, nx):
        gather(d).start()
    hand_over(0).start()
    for d in range(1, nx):
        gather(d).wait_recv()
        hand_over(d).start()

    arrived(COTS, cots_r)

    def order_cots(g, _):
        part = cots_r[pl.ds(g * GROUP, GROUP)].astype(F32).reshape(GROUP * cot_block, half)
        part = dot(fold[...], part.astype(BF16)).astype(BF16)
        for h in range(HALVES):
            cot_mat[pl.ds(g * span, span), h * half : (h + 1) * half] = part[h * span : (h + 1) * span]
        return 0

    lax.fori_loop(0, groups, order_cots, 0)
    arrived(ROWS, rows_r)
    spread(M1, lambda e: m1.at[:, e], lambda s: m1_r.at[:, s])
    spread(M2, lambda e: m2.at[:, e], lambda s: m2_r.at[:, s])

    def order_rows(g, _):
        part = rows_r[pl.ds(g * GROUP, GROUP)].reshape(GROUP * block, quarter)
        part = dot(swap[...], part).astype(BF16)
        for q in range(QUARTERS):
            x_mat[pl.ds(g * span, span), q * quarter : (q + 1) * quarter] = part[q * span : (q + 1) * span]
        return 0

    lax.fori_loop(0, groups, order_rows, 0)

    for d in range(nx):
        hand_over(d).wait_recv()

    tile = min(256, hidden)
    for t in range(hidden // tile):
        at = t * tile
        gate_w = jnp.concatenate([full_w[j, at : at + tile] for j in range(nx * CORES)], axis=1)
        pre_gate = dot(x_mat[...], gate_w, ((1,), (1,)))
        at += hidden
        up_w = jnp.concatenate([full_w[j, at : at + tile] for j in range(nx * CORES)], axis=1)
        pre_up = dot(x_mat[...], up_w, ((1,), (1,)))
        at -= hidden
        s = jax.nn.sigmoid(pre_gate)
        upstream = cot_mat[:, at : at + tile].astype(F32)
        grad_up = upstream * pre_gate * s
        grad_gate = upstream * pre_up * s * (1.0 + pre_gate * (1.0 - s))
        pair[:, at : at + tile] = grad_gate.astype(BF16)
        pair[:, hidden + at : hidden + at + tile] = grad_up.astype(BF16)
        pair_t[at : at + tile, :] = grad_gate.T.astype(BF16)
        pair_t[hidden + at : hidden + at + tile, :] = grad_up.T.astype(BF16)

    per_quarter = nx * CORES // QUARTERS
    for q in range(QUARTERS):
        parts = [dot(pair[...], full_w[q * per_quarter + i]) for i in range(per_quarter)]
        part = jnp.concatenate(parts, axis=1).astype(BF16)
        for g in range(groups):
            rows_r[g * GROUP + q] = part[g * span : (g + 1) * span]

    left(COTS, cots_s.at[pl.ds(0, n - 1)])
    left(ROWS, rows_s.at[pl.ds(0, n - 1)])

    def order_back(g, _):
        part = rows_r[pl.ds(g * GROUP, GROUP)].reshape(GROUP * block, quarter)
        part = dot(swap[...], part).astype(BF16)
        rows_s[pl.ds(g * GROUP, GROUP)] = part.reshape(GROUP, block, quarter)
        return 0

    lax.fori_loop(0, groups, order_back, 0)
    spread(BACK, lambda e: rows_s.at[e], lambda s: back_r.at[s])

    chunk = min(384, 2 * hidden)

    def weight_grad(j):
        at = pl.multiple_of(j * cols, cols)

        def rows_of(r, _):
            spot = pl.ds(pl.multiple_of(r * chunk, chunk), chunk)
            grads[j, spot, :] = dot(pair_t[spot, :], x_mat[:, pl.ds(at, cols)]).astype(BF16)
            return 0

        lax.fori_loop(0, 2 * hidden // chunk, rows_of, 0)

    def halve(d):
        return pltpu.make_async_remote_copy(
            src_ref=grads.at[lax.rem(x + d, nx) * CORES + 1 - core],
            dst_ref=half_r.at[d - 1],
            send_sem=half_send.at[d - 1],
            recv_sem=half_recv.at[d - 1],
            device_id=(twin, me),
            device_id_type=MESH,
        )

    def pass_on(d):
        return pltpu.make_async_remote_copy(
            src_ref=grads.at[x_peer(d)],
            dst_ref=quarter_r.at[d - 1],
            send_sem=sum_send.at[d - 1],
            recv_sem=sum_recv.at[d - 1],
            device_id=(x_peer(d), me),
            device_id_type=MESH,
        )

    for d in range(1, nx + 1):
        weight_grad(lax.rem(x + d, nx) * CORES + 1 - core)
        halve(d).start()
    for d in range(1, nx + 1):
        weight_grad(x_peer(d))
        halve(d).wait_recv()
        if d < nx:

            def add(r, _):
                spot = pl.ds(pl.multiple_of(r * chunk, chunk), chunk)
                both = grads[x_peer(d), spot, :].astype(F32) + half_r[d - 1, spot, :].astype(F32)
                grads[x_peer(d), spot, :] = both.astype(BF16)
                return 0

            lax.fori_loop(0, 2 * hidden // chunk, add, 0)
            pass_on(d).start()

    for d in range(1, nx):
        pass_on(d).wait_recv()
    arrived(M1, m1_r)
    arrived(M2, m2_r)

    rows = GROUP * per_source

    def adam(i, _):
        for a in range(2):
            spot = pl.ds(a * hidden + i * rows, rows)
            total = grads[dp, spot, :].astype(F32) + half_r[nx - 1, spot, :].astype(F32)
            for d in range(nx - 1):
                total += quarter_r[d, spot, :].astype(F32)
            gradient = total * (1.0 / loss_scale)
            first = m1_r[a, pl.ds(i * GROUP, GROUP)].astype(F32).reshape(rows, cols)
            second = m2_r[a, pl.ds(i * GROUP, GROUP)].astype(F32).reshape(rows, cols)
            first = beta_one * first + (1.0 - beta_one) * gradient
            second = beta_two * second + (1.0 - beta_two) * gradient * gradient
            weight = full_w[dp, spot, :].astype(F32)
            weight = weight - step_size * first / (jnp.sqrt(second) + adam_eps)
            out = pl.ds(i * rows, rows)
            w_out[a, out, :] = weight.astype(BF16)
            m1_out[a, out, :] = first.astype(BF16)
            m2_out[a, out, :] = second.astype(BF16)
        return 0

    lax.fori_loop(0, groups, adam, 0)

    ids = lax.broadcasted_iota(jnp.int32, (tok, experts), 1)
    route_cols = [routes_col[:, k : k + 1] for k in range(2)]
    hot = [(ids == r).astype(F32) for r in route_cols]
    before = dot((earlier > later).astype(BF16), (hot[0] + hot[1]).astype(BF16))
    spots = [
        r * block + jnp.sum(h * before, axis=1, keepdims=True).astype(jnp.int32)
        for r, h in zip(route_cols, hot)
    ]
    piece = lax.broadcasted_iota(jnp.int32, (tok, n * block), 1)

    arrived(BACK, back_r)
    returned = back_r[...].reshape(n * block, quarter)
    for q in range(QUARTERS):
        pick = (piece == spots[0] + q * cap) | (piece == spots[1] + q * cap)
        token_out[:, q * quarter : (q + 1) * quarter] = dot(pick.astype(BF16), returned).astype(BF16)

    for d in range(1, nx):
        gather(d).wait_send()
        pass_on(d).wait_send()
    for d in range(nx):
        hand_over(d).wait_send()
        halve(d + 1).wait_send()
    left(M1, m1_r.at[:, pl.ds(0, n - 1)])
    left(M2, m2_r.at[:, pl.ds(0, n - 1)])
    left(BACK, rows_s.at[pl.ds(0, n - 1)])


def swap_matrix(outer, inner, cap):
    size = outer * inner * cap
    order = np.arange(size).reshape(inner, outer, cap).transpose(1, 0, 2).reshape(-1)
    matrix = np.zeros((size, size), np.float32)
    matrix[np.arange(size), order] = 1.0
    return jnp.asarray(matrix, BF16)


def per_device(
    mesh_sizes, tokens, routes, router_gates, hidden_cotangent, weights, first_moment, second_moment
):
    ndp, n = mesh_sizes
    nx = ndp // CORES
    nz = min(8, n)
    ny = n // nz
    tok, width = tokens.shape
    hidden = hidden_cotangent.shape[2]
    cap = 3 * tok * 2 // (2 * n)
    per_source, cols = weights.shape[2], weights.shape[3]
    gate_factor = router_gates.astype(F32) / gate_unit
    scaled = (gate_factor[:, :, None] * hidden_cotangent.astype(F32)).astype(BF16)
    scaled = scaled.reshape(tok, 2 * hidden)
    block, cot_block, slots = QUARTERS * cap, HALVES * cap, n * cap
    vmem = pl.BlockSpec(memory_space=pltpu.VMEM)
    hbm = pl.BlockSpec(memory_space=pl.ANY)
    state = jax.ShapeDtypeStruct((2, hidden, cols), BF16)
    dma = pltpu.SemaphoreType.DMA
    token_grads, new_w, new_first, new_second = pl.pallas_call(
        functools.partial(kernel, nx, ny, nz, cap),
        out_shape=(jax.ShapeDtypeStruct((tok, width), BF16), state, state, state),
        in_specs=[vmem] * 6 + [hbm] * 3,
        out_specs=(vmem,) * 4,
        scratch_shapes=[
            pltpu.VMEM((n, block, width // QUARTERS), BF16),
            pltpu.VMEM((n, block, width // QUARTERS), BF16),
            pltpu.VMEM((n, cot_block, hidden // HALVES), BF16),
            pltpu.VMEM((n, cot_block, hidden // HALVES), BF16),
            pltpu.VMEM((2, n, per_source, cols), BF16),
            pltpu.VMEM((2, n, per_source, cols), BF16),
            pltpu.VMEM((2, n, per_source, cols), BF16),
            pltpu.VMEM((ndp, 2 * hidden, cols), BF16),
            pltpu.VMEM((slots, width), BF16),
            pltpu.VMEM((slots, hidden), BF16),
            pltpu.VMEM((slots, 2 * hidden), BF16),
            pltpu.VMEM((2 * hidden, slots), BF16),
            pltpu.VMEM((n, block, width // QUARTERS), BF16),
            pltpu.VMEM((ndp, 2 * hidden, cols), BF16),
            pltpu.VMEM((nx, 2 * hidden, cols), BF16),
            pltpu.VMEM((nx - 1, 2 * hidden, cols), BF16),
            dma((6,)),
            dma((6,)),
            dma((nx - 1,)),
            dma((nx - 1,)),
            dma((nx,)),
            dma((nx,)),
            dma((nx,)),
            dma((nx,)),
            dma((nx - 1,)),
            dma((nx - 1,)),
        ],
        compiler_params=pltpu.CompilerParams(
            collective_id=0, has_side_effects=True, vmem_limit_bytes=60 * 1024 * 1024
        ),
        name="experts_step",
    )(
        routes.T,
        routes,
        tokens,
        scaled,
        swap_matrix(QUARTERS, GROUP, cap),
        swap_matrix(HALVES, GROUP, cap),
        weights,
        first_moment,
        second_moment,
    )
    shape = (2, 1, hidden, cols)
    return token_grads, new_w.reshape(shape), new_first.reshape(shape), new_second.reshape(shape)


def solution(mesh):
    placed = (
        P(("dp", "expert"), None),
        P(("dp", "expert"), None),
        P(("dp", "expert"), None),
        P(("dp", "expert"), None, None),
        P(None, None, "expert", "dp"),
        P(None, None, "expert", "dp"),
        P(None, None, "expert", "dp"),
    )
    return jax.shard_map(
        functools.partial(per_device, (mesh.shape["dp"], mesh.shape["expert"])),
        mesh=mesh,
        in_specs=placed,
        out_specs=(
            P(("dp", "expert"), None),
            P(None, "expert", None, "dp"),
            P(None, "expert", None, "dp"),
            P(None, "expert", None, "dp"),
        ),
        check_vma=False,
    )
```

time: 399 us -> 224 us (0.56)
  Pallas kernels: 0 us -> 212 us
  waiting for transfers between devices: 203 us -> 0 us
  local copies, waits for them, and re-layouts: 70.7 us -> 8.88 us
  blocking collectives: 44.2 us -> 0 us
  matrix products: 25.6 us -> 0 us
  starting transfers between devices: 24.6 us -> 0 us
  between operations: 14.3 us -> 0.66 us
  other arithmetic: 15.1 us -> 2.06 us
    pallas_call x0 -> x1, Pallas kernels: none -> 212 us  [per_device(): pl.pallas_call(functools.partial(kernel, nx, ny, nz, cap), out_shape=(jax...]
    all_to_all x5 -> x0, waiting for transfers between devices: 203 us -> none  [the longest x1 72 us: per_device(): lax.all_to_all(send_rows, 'expert', split_axis=0, concat_axis=0, tiled=True)]
    all_to_all x1 -> x0, blocking collectives: 44.2 us -> none  [per_device(): lax.all_to_all(weights, 'expert', split_axis=1, concat_axis=2, tiled=True)]
    unnamed x28 -> x12, local copies, waits for them, and re-layouts: 45.1 us -> 8.77 us
    dot_general x4 -> x0, matrix products: 25.6 us -> none  [the longest x1 9.3 us: per_device(): jnp.einsum('rah,ahd->rd', paired, full_weights, preferred_element_type=jn...]
    all_to_all x5 -> x0, starting transfers between devices: 24.3 us -> none  [the longest x1 5.34 us: per_device(): lax.all_to_all(backward, 'expert', split_axis=0, concat_axis=0, tiled=True)]
    reshape x4 -> x0, local copies, waits for them, and re-layouts: 11.5 us -> none  [the longest x1 4.28 us: per_device(): flat_rows = rows_in.reshape(sources * slots_in, model_width)]
    gather x4 -> x0, local copies, waits for them, and re-layouts: 7.57 us -> none  [the longest x2 5.28 us: per_device(): jnp.take(tokens, token_index, axis=0)]
  transfers between devices with their start and end apart: 7 -> 0, of which waited for: 5 -> 0; matrix products, arithmetic and copies ran while one was open for 12% -> 0% of each run, Pallas kernels for 0% -> 0%
where the time goes in v1:
time: 224 us
  Pallas kernels  212 us (95%)
  local copies, waits for them, and re-layouts  8.88 us (4%)
    pallas_call x1, Pallas kernels, per_device(): pl.pallas_call(functools.partial(kernel, nx, ny, nz, cap), out_shape=(jax...  212 us
    unnamed x12, local copies, waits for them, and re-layouts  8.77 us

profile of v1, /device:TPU:6, one launch (start us, length us, event | category | flops | bytes accessed | tf_op | source)
XLA Modules:
  0.0 223.7 jit_solution(9138160085859949695)
XLA Ops:
  0.6 0.7 convert_multiply_fusion
  1.3 0.1 copy.13
  1.4 1.4 copy.14.routes_col
  2.8 1.4 multiply_convert_fusion
  4.2 0.8 copy.18
  5.0 212.1 %experts_step.1 = (bf16[128,3072]{1,0:T(8,128)(2,1)}, bf16[2,768,384]{2,1,0:T(8,128)(2,1)}, bf16[2,768,384]{2,1,0:T(8,128)(2,1)}, bf16[2,768,384]{2,1,0:T(8,128)(2,1)}) custom-call(s32[2,128]{1,0:T(2,128)} %bitcast.17, s32[128,2]{1,0:T(8,128)} %copy.14.routes_col, bf16[128,3072]{1,0:T(8,128)(2,1)} %tokens.1, bf16[128,1536]{1,0:T(8,128)(2,1)} %bitcast.13, ...), custom_call_target="tpu_custom_call" | custom-call | tf_op jit(solution)/shard_map/experts_step/pallas_call | solution.py:404
  217.1 0.0 copy-start.2
  217.1 2.2 copy.23
  219.2 0.0 copy-done.2
  219.3 0.0 copy-start.1
  219.3 1.0 copy.24
  220.3 0.7 copy-done.1
  220.9 0.0 copy-start
  220.9 1.0 copy.25
  222.0 0.7 copy-done
  222.6 1.0 copy.26
Async XLA Ops:
  217.1 2.2 copy-start.2
  219.3 1.7 copy-start.1
  220.9 1.7 copy-start

commit v2 on v1

--- a/solution.py
+++ b/solution.py
@@ -2,7 +2,6 @@
 
 import jax
 import jax.numpy as jnp
-import numpy as np
 from jax import lax
 from jax.experimental import pallas as pl
 from jax.experimental.pallas import tpu as pltpu
@@ -29,17 +28,25 @@
     return lax.dot_general(a, b, (dims, ((), ())), preferred_element_type=F32)
 
 
+def order_matrix(outer, inner, cap):
+    size = outer * inner * cap
+    row = lax.broadcasted_iota(jnp.int32, (size, size), 0)
+    source = lax.broadcasted_iota(jnp.int32, (size, size), 1)
+    a = sum((row >= i * inner * cap).astype(jnp.int32) for i in range(1, outer))
+    rest = row - a * (inner * cap)
+    b = sum((rest >= i * cap).astype(jnp.int32) for i in range(1, inner))
+    return (source == b * (outer * cap) + a * cap + rest - b * cap).astype(BF16)
+
+
 def kernel(
     nx,
     ny,
     nz,
     cap,
-    routes_row,
-    routes_col,
+    routes,
+    gates,
     tokens,
-    scaled,
-    swap,
-    fold,
+    cotangent,
     w,
     m1,
     m2,
@@ -51,6 +58,7 @@
     rows_r,
     cots_s,
     cots_r,
+    scaled,
     w_r,
     m1_r,
     m2_r,
@@ -63,6 +71,8 @@
     grads,
     half_r,
     quarter_r,
+    swap,
+    fold,
     send,
     recv,
     gather_send,
@@ -80,7 +90,7 @@
     y, z = me // nz, me % nz
     twin = x * CORES + 1 - core
     tok, width = tokens.shape
-    hidden = scaled.shape[1] // 2
+    hidden = cotangent.shape[2]
     quarter, half = width // QUARTERS, hidden // HALVES
     per_source, cols = w.shape[2], w.shape[3]
     block = QUARTERS * cap
@@ -90,7 +100,9 @@
     slots = n * cap
 
     def peer(i):
-        return lax.rem(y + i // nz, ny) * nz + lax.rem(z + i % nz, nz)
+        step = i // ny
+        dz = jnp.where(step % 2 == 1, (step + 1) // 2, nz - step // 2)
+        return lax.rem(y + i % ny, ny) * nz + lax.rem(z + dz, nz)
 
     def x_peer(d):
         return lax.rem(x + d, nx) * CORES + core
@@ -107,7 +119,7 @@
     pl.semaphore_signal(barrier, inc=1, device_id=(twin, me), device_id_type=MESH)
     pl.semaphore_wait(barrier, n - 1 + nx - 1 + 1)
 
-    def spread(kind, source, landing):
+    def spread(kind, source, landing, parts=((ny, n), (1, ny))):
         def start(i, _):
             to = peer(i)
             pltpu.make_async_remote_copy(
@@ -120,7 +132,8 @@
             ).start()
             return 0
 
-        lax.fori_loop(1, n, start, 0)
+        for first, last in parts:
+            lax.fori_loop(first, last, start, 0)
         pltpu.make_async_copy(source(me), landing(me), recv.at[kind]).start()
 
     def arrived(kind, ref):
@@ -135,22 +148,26 @@
     earlier = lax.broadcasted_iota(jnp.int32, (tok, tok), 0)
     later = lax.broadcasted_iota(jnp.int32, (tok, tok), 1)
     ids = lax.broadcasted_iota(jnp.int32, (experts, tok), 0)
-    route_rows = [routes_row[k : k + 1, :] for k in range(2)]
+    route_rows = [routes[k : k + 1, :] for k in range(2)]
     hot = [(ids == r).astype(F32) for r in route_rows]
     before = dot((hot[0] + hot[1]).astype(BF16), (earlier < later).astype(BF16))
     pos_row = [jnp.sum(h * before, axis=0, keepdims=True).astype(jnp.int32) for h in hot]
 
+    def column(row):
+        return jnp.sum(jnp.where(earlier == later, row, jnp.zeros_like(row)), axis=1, keepdims=True)
+
+    spots = [column(r * block + p) for r, p in zip(route_rows, pos_row)]
+    for k in range(2):
+        factor = column(gates[k : k + 1, :].astype(F32)) * (1.0 / gate_unit)
+        scaled[:, k * hidden : (k + 1) * hidden] = (factor * cotangent[:, k, :].astype(F32)).astype(BF16)
+
+    swap[...] = order_matrix(QUARTERS, GROUP, cap)
+    fold[...] = order_matrix(HALVES, GROUP, cap)
+
     piece = lax.broadcasted_iota(jnp.int32, (GROUP * block, tok), 0)
     cot_piece = lax.broadcasted_iota(jnp.int32, (GROUP * cot_block, tok), 0)
 
-    def pack(g, _):
-        first = g * (GROUP * block)
-        total = jnp.zeros((GROUP * block, quarter), F32)
-        for q in range(QUARTERS):
-            spot = [r * block + p + q * cap - first for r, p in zip(route_rows, pos_row)]
-            pick = (piece == spot[0]) | (piece == spot[1])
-            total += dot(pick.astype(BF16), tokens[:, q * quarter : (q + 1) * quarter])
-        rows_s[pl.ds(g * GROUP, GROUP)] = total.astype(BF16).reshape(GROUP, block, quarter)
+    def pack_cots(g, _):
         first = g * (GROUP * cot_block)
         total = jnp.zeros((GROUP * cot_block, half), F32)
         for k in range(2):
@@ -162,10 +179,21 @@
         cots_s[pl.ds(g * GROUP, GROUP)] = total.reshape(GROUP, cot_block, half).astype(BF16)
         return 0
 
-    lax.fori_loop(0, groups, pack, 0)
+    def pack_rows(g, _):
+        first = g * (GROUP * block)
+        total = jnp.zeros((GROUP * block, quarter), F32)
+        for q in range(QUARTERS):
+            spot = [r * block + p + q * cap - first for r, p in zip(route_rows, pos_row)]
+            pick = (piece == spot[0]) | (piece == spot[1])
+            total += dot(pick.astype(BF16), tokens[:, q * quarter : (q + 1) * quarter])
+        rows_s[pl.ds(g * GROUP, GROUP)] = total.astype(BF16).reshape(GROUP, block, quarter)
+        return 0
+
+    lax.fori_loop(0, groups, pack_cots, 0)
+    spread(COTS, lambda e: cots_s.at[e], lambda s: cots_r.at[s])
+    lax.fori_loop(0, groups, pack_rows, 0)
 
     left(W, w_r.at[:, pl.ds(0, n - 1)])
-    spread(COTS, lambda e: cots_s.at[e], lambda s: cots_r.at[s])
     spread(ROWS, lambda e: rows_s.at[e], lambda s: rows_r.at[s])
 
     arrived(W, w_r)
@@ -217,9 +245,11 @@
         return 0
 
     lax.fori_loop(0, groups, order_cots, 0)
-    arrived(ROWS, rows_r)
+    left(COTS, cots_s.at[pl.ds(0, n - 1)])
+    left(ROWS, rows_s.at[pl.ds(0, n - 1)])
     spread(M1, lambda e: m1.at[:, e], lambda s: m1_r.at[:, s])
     spread(M2, lambda e: m2.at[:, e], lambda s: m2_r.at[:, s])
+    arrived(ROWS, rows_r)
 
     def order_rows(g, _):
         part = rows_r[pl.ds(g * GROUP, GROUP)].reshape(GROUP * block, quarter)
@@ -258,9 +288,6 @@
         for g in range(groups):
             rows_r[g * GROUP + q] = part[g * span : (g + 1) * span]
 
-    left(COTS, cots_s.at[pl.ds(0, n - 1)])
-    left(ROWS, rows_s.at[pl.ds(0, n - 1)])
-
     def order_back(g, _):
         part = rows_r[pl.ds(g * GROUP, GROUP)].reshape(GROUP * block, quarter)
         part = dot(swap[...], part).astype(BF16)
@@ -347,14 +374,6 @@
 
     lax.fori_loop(0, groups, adam, 0)
 
-    ids = lax.broadcasted_iota(jnp.int32, (tok, experts), 1)
-    route_cols = [routes_col[:, k : k + 1] for k in range(2)]
-    hot = [(ids == r).astype(F32) for r in route_cols]
-    before = dot((earlier > later).astype(BF16), (hot[0] + hot[1]).astype(BF16))
-    spots = [
-        r * block + jnp.sum(h * before, axis=1, keepdims=True).astype(jnp.int32)
-        for r, h in zip(route_cols, hot)
-    ]
     piece = lax.broadcasted_iota(jnp.int32, (tok, n * block), 1)
 
     arrived(BACK, back_r)
@@ -374,12 +393,15 @@
     left(BACK, rows_s.at[pl.ds(0, n - 1)])
 
 
-def swap_matrix(outer, inner, cap):
-    size = outer * inner * cap
-    order = np.arange(size).reshape(inner, outer, cap).transpose(1, 0, 2).reshape(-1)
-    matrix = np.zeros((size, size), np.float32)
-    matrix[np.arange(size), order] = 1.0
-    return jnp.asarray(matrix, BF16)
+def place(*refs):
+    count = (len(refs) - 1) // 2
+    copies = [
+        pltpu.make_async_copy(refs[i], refs[count + i], refs[-1].at[i]) for i in range(count)
+    ]
+    for copy in copies:
+        copy.start()
+    for copy in copies:
+        copy.wait()
 
 
 def per_device(
@@ -393,24 +415,22 @@
     hidden = hidden_cotangent.shape[2]
     cap = 3 * tok * 2 // (2 * n)
     per_source, cols = weights.shape[2], weights.shape[3]
-    gate_factor = router_gates.astype(F32) / gate_unit
-    scaled = (gate_factor[:, :, None] * hidden_cotangent.astype(F32)).astype(BF16)
-    scaled = scaled.reshape(tok, 2 * hidden)
     block, cot_block, slots = QUARTERS * cap, HALVES * cap, n * cap
     vmem = pl.BlockSpec(memory_space=pltpu.VMEM)
     hbm = pl.BlockSpec(memory_space=pl.ANY)
-    state = jax.ShapeDtypeStruct((2, hidden, cols), BF16)
+    shapes = [(tok, width)] + [(2, hidden, cols)] * 3
     dma = pltpu.SemaphoreType.DMA
-    token_grads, new_w, new_first, new_second = pl.pallas_call(
+    results = pl.pallas_call(
         functools.partial(kernel, nx, ny, nz, cap),
-        out_shape=(jax.ShapeDtypeStruct((tok, width), BF16), state, state, state),
-        in_specs=[vmem] * 6 + [hbm] * 3,
+        out_shape=tuple(pltpu.VMEM(shape, BF16) for shape in shapes),
+        in_specs=[vmem] * 4 + [hbm] * 3,
         out_specs=(vmem,) * 4,
         scratch_shapes=[
             pltpu.VMEM((n, block, width // QUARTERS), BF16),
             pltpu.VMEM((n, block, width // QUARTERS), BF16),
             pltpu.VMEM((n, cot_block, hidden // HALVES), BF16),
             pltpu.VMEM((n, cot_block, hidden // HALVES), BF16),
+            pltpu.VMEM((tok, 2 * hidden), BF16),
             pltpu.VMEM((2, n, per_source, cols), BF16),
             pltpu.VMEM((2, n, per_source, cols), BF16),
             pltpu.VMEM((2, n, per_source, cols), BF16),
@@ -423,6 +443,8 @@
             pltpu.VMEM((ndp, 2 * hidden, cols), BF16),
             pltpu.VMEM((nx, 2 * hidden, cols), BF16),
             pltpu.VMEM((nx - 1, 2 * hidden, cols), BF16),
+            pltpu.VMEM((GROUP * block,) * 2, BF16),
+            pltpu.VMEM((GROUP * cot_block,) * 2, BF16),
             dma((6,)),
             dma((6,)),
             dma((nx - 1,)),
@@ -435,20 +457,27 @@
             dma((nx - 1,)),
         ],
         compiler_params=pltpu.CompilerParams(
-            collective_id=0, has_side_effects=True, vmem_limit_bytes=60 * 1024 * 1024
+            collective_id=0, has_side_effects=True, vmem_limit_bytes=50 * 1024 * 1024
         ),
         name="experts_step",
     )(
         routes.T,
-        routes,
+        router_gates.T,
         tokens,
-        scaled,
-        swap_matrix(QUARTERS, GROUP, cap),
-        swap_matrix(HALVES, GROUP, cap),
+        hidden_cotangent,
         weights,
         first_moment,
         second_moment,
     )
+    token_grads, new_w, new_first, new_second = pl.pallas_call(
+        place,
+        out_shape=tuple(jax.ShapeDtypeStruct(shape, BF16) for shape in shapes),
+        in_specs=[vmem] * 4,
+        out_specs=(hbm,) * 4,
+        scratch_shapes=[dma((4,))],
+        compiler_params=pltpu.CompilerParams(vmem_limit_bytes=1024 * 1024),
+        name="place",
+    )(*(pltpu.with_memory_space_constraint(result, pltpu.VMEM) for result in results))
     shape = (2, 1, hidden, cols)
     return token_grads, new_w.reshape(shape), new_first.reshape(shape), new_second.reshape(shape)
 

time: 224 us -> 210 us (0.938)
  local copies, waits for them, and re-layouts: 8.88 us -> 0 us
  Pallas kernels: 212 us -> 208 us
    unnamed x12 -> x0, local copies, waits for them, and re-layouts: 8.77 us -> none
    pallas_call x1 -> x2, Pallas kernels: 212 us -> 208 us  [the longest x1 206 us: per_device(): pl.pallas_call(functools.partial(kernel, nx, ny, nz, cap), out_shape=tupl...]
where the time goes in v2:
time: 210 us; the launch traced here: 209 us
  Pallas kernels  208 us (99%)
    pallas_call x1, Pallas kernels, per_device(): pl.pallas_call(functools.partial(kernel, nx, ny, nz, cap), out_shape=tupl...  206 us

profile of v2, /device:TPU:6, one launch (start us, length us, event | category | flops | bytes accessed | tf_op | source)
XLA Modules:
  0.0 209.0 jit_solution(13804789835427140900)
XLA Ops:
  0.6 206.3 %experts_step.1 = (bf16[128,3072]{1,0:T(8,128)(2,1)S(1)}, bf16[2,768,384]{2,1,0:T(8,128)(2,1)S(1)}, bf16[2,768,384]{2,1,0:T(8,128)(2,1)S(1)}, bf16[2,768,384]{2,1,0:T(8,128)(2,1)S(1)}) custom-call(s32[2,128]{1,0:T(2,128)} %bitcast.11, s32[2,128]{1,0:T(2,128)} %bitcast.12, bf16[128,3072]{1,0:T(8,128)(2,1)} %tokens.1, bf16[128,2,768]{2,1,0:T(2,128)(2,1)} %cotangent.1, ...), custom_call_target="tpu_custom_call" | custom-call | tf_op jit(solution)/shard_map/experts_step/pallas_call | solution.py:423
  207.0 2.1 place.1

commit v3 on v2

--- a/solution.py
+++ b/solution.py
@@ -20,8 +20,9 @@
 CORES = 2
 QUARTERS = 4
 HALVES = 2
+ALONG_Z = 8
 GROUP = 4
-W, ROWS, COTS, M1, M2, BACK = range(6)
+W, ROWS, COTS, M1, M2, LONG, SHORT, OWN = range(8)
 
 
 def dot(a, b, dims=((1,), (0,))):
@@ -73,6 +74,16 @@
     quarter_r,
     swap,
     fold,
+    near_tokens,
+    near_routes,
+    near_back,
+    picks_own,
+    picks_far,
+    picks_short,
+    near_send,
+    near_recv,
+    bring_send,
+    bring_recv,
     send,
     recv,
     gather_send,
@@ -144,19 +155,48 @@
 
     spread(W, lambda e: w.at[:, e], lambda s: w_r.at[:, s])
 
+    side = 1 - 2 * core
+    far = nz // 2
+    short = nz - 1 - far
+
+    def plane(step):
+        return lax.rem(z + step + 2 * nz, nz)
+
+    def lend(i):
+        to = (dp, y * nz + plane(side * (1 - 2 * i)))
+        return [
+            pltpu.make_async_remote_copy(
+                src_ref=source,
+                dst_ref=landing.at[i],
+                send_sem=near_send.at[2 * j + i],
+                recv_sem=near_recv.at[2 * j + i],
+                device_id=to,
+                device_id_type=MESH,
+            )
+            for j, (source, landing) in enumerate(((tokens, near_tokens), (routes, near_routes)))
+        ]
+
+    for i in range(2):
+        for copy in lend(i):
+            copy.start()
+    picks_of = (picks_far, picks_short)
+
     experts = n
     earlier = lax.broadcasted_iota(jnp.int32, (tok, tok), 0)
     later = lax.broadcasted_iota(jnp.int32, (tok, tok), 1)
     ids = lax.broadcasted_iota(jnp.int32, (experts, tok), 0)
-    route_rows = [routes[k : k + 1, :] for k in range(2)]
-    hot = [(ids == r).astype(F32) for r in route_rows]
-    before = dot((hot[0] + hot[1]).astype(BF16), (earlier < later).astype(BF16))
-    pos_row = [jnp.sum(h * before, axis=0, keepdims=True).astype(jnp.int32) for h in hot]
+
+    def number(ref):
+        rows = [ref[k : k + 1, :] for k in range(2)]
+        hot = [(ids == r).astype(F32) for r in rows]
+        before = dot((hot[0] + hot[1]).astype(BF16), (earlier < later).astype(BF16))
+        return rows, [jnp.sum(h * before, axis=0, keepdims=True).astype(jnp.int32) for h in hot]
+
+    route_rows, pos_row = number(routes)
 
     def column(row):
         return jnp.sum(jnp.where(earlier == later, row, jnp.zeros_like(row)), axis=1, keepdims=True)
 
-    spots = [column(r * block + p) for r, p in zip(route_rows, pos_row)]
     for k in range(2):
         factor = column(gates[k : k + 1, :].astype(F32)) * (1.0 / gate_unit)
         scaled[:, k * hidden : (k + 1) * hidden] = (factor * cotangent[:, k, :].astype(F32)).astype(BF16)
@@ -164,7 +204,7 @@
     swap[...] = order_matrix(QUARTERS, GROUP, cap)
     fold[...] = order_matrix(HALVES, GROUP, cap)
 
-    piece = lax.broadcasted_iota(jnp.int32, (GROUP * block, tok), 0)
+    piece = lax.broadcasted_iota(jnp.int32, (ny * block, tok), 0)
     cot_piece = lax.broadcasted_iota(jnp.int32, (GROUP * cot_block, tok), 0)
 
     def pack_cots(g, _):
@@ -179,23 +219,56 @@
         cots_s[pl.ds(g * GROUP, GROUP)] = total.reshape(GROUP, cot_block, half).astype(BF16)
         return 0
 
-    def pack_rows(g, _):
-        first = g * (GROUP * block)
-        total = jnp.zeros((GROUP * block, quarter), F32)
+    def pack_rows(first, count, sign, numbers, rows, picks):
+        places = []
+        for k, (r, p) in enumerate(zip(*numbers)):
+            at_y = sum((r >= i * nz).astype(jnp.int32) for i in range(1, ny))
+            places.append((r - at_y * nz, at_y * block + p))
+        spots = []
+        for at_z, at in places:
+            step = sign * (at_z - z)
+            step = jnp.where(step < 0, step + nz, step)
+            spots.append(column(jnp.where(step < count, step * (ny * block) + at, -nz * ny * block)))
+        position = lax.broadcasted_iota(jnp.int32, (tok, count * ny * block), 1)
         for q in range(QUARTERS):
-            spot = [r * block + p + q * cap - first for r, p in zip(route_rows, pos_row)]
-            pick = (piece == spot[0]) | (piece == spot[1])
-            total += dot(pick.astype(BF16), tokens[:, q * quarter : (q + 1) * quarter])
-        rows_s[pl.ds(g * GROUP, GROUP)] = total.astype(BF16).reshape(GROUP, block, quarter)
-        return 0
+            pick = (position == spots[0] + q * cap) | (position == spots[1] + q * cap)
+            picks[q] = pick.astype(BF16)
+
+        def pack(g, _):
+            goal = plane(sign * g)
+            total = jnp.zeros((ny * block, quarter), F32)
+            for q in range(QUARTERS):
+                spot = [jnp.where(at_z == goal, at + q * cap, -1) for at_z, at in places]
+                pick = (piece == spot[0]) | (piece == spot[1])
+                total += dot(pick.astype(BF16), rows[:, q * quarter : (q + 1) * quarter])
+            rows_s[pl.ds((first + g) * ny, ny)] = total.astype(BF16).reshape(ny, block, quarter)
+            return 0
+
+        lax.fori_loop(0, count, pack, 0)
+
+    def send_rows(first, count, sign, source_z):
+        source = y * nz + source_z
+
+        def start(g, i):
+            at_y = lax.rem(y + i, ny)
+            pltpu.make_async_remote_copy(
+                src_ref=rows_s.at[(first + g) * ny + at_y],
+                dst_ref=rows_r.at[source],
+                send_sem=send.at[ROWS],
+                recv_sem=recv.at[ROWS],
+                device_id=(dp, at_y * nz + plane(sign * g)),
+                device_id_type=MESH,
+            ).start()
+            return 0
+
+        lax.fori_loop(ny, count * ny, lambda i, _: start(i // ny, i % ny), 0)
+        lax.fori_loop(1, ny, lambda i, _: start(0, i), 0)
+        pltpu.make_async_copy(rows_s.at[first * ny + y], rows_r.at[source], recv.at[ROWS]).start()
 
     lax.fori_loop(0, groups, pack_cots, 0)
     spread(COTS, lambda e: cots_s.at[e], lambda s: cots_r.at[s])
-    lax.fori_loop(0, groups, pack_rows, 0)
-
-    left(W, w_r.at[:, pl.ds(0, n - 1)])
-    spread(ROWS, lambda e: rows_s.at[e], lambda s: rows_r.at[s])
-
+    pack_rows(0, 1, 1, (route_rows, pos_row), tokens, picks_own)
+    send_rows(0, 1, 0, z)
     arrived(W, w_r)
 
     def own_columns(i, _):
@@ -231,6 +304,14 @@
     for d in range(1, nx):
         gather(d).start()
     hand_over(0).start()
+
+    for i, (first, count, sign) in enumerate(((1, far, side), (1 + far, short, -side))):
+        for copy in lend(i):
+            copy.wait_recv()
+        pack_rows(first, count, sign, number(near_routes.at[i]), near_tokens.at[i], picks_of[i])
+        send_rows(first, count, sign, plane(-sign))
+    spread(M1, lambda e: m1.at[:, e], lambda s: m1_r.at[:, s])
+
     for d in range(1, nx):
         gather(d).wait_recv()
         hand_over(d).start()
@@ -245,10 +326,6 @@
         return 0
 
     lax.fori_loop(0, groups, order_cots, 0)
-    left(COTS, cots_s.at[pl.ds(0, n - 1)])
-    left(ROWS, rows_s.at[pl.ds(0, n - 1)])
-    spread(M1, lambda e: m1.at[:, e], lambda s: m1_r.at[:, s])
-    spread(M2, lambda e: m2.at[:, e], lambda s: m2_r.at[:, s])
     arrived(ROWS, rows_r)
 
     def order_rows(g, _):
@@ -288,6 +365,10 @@
         for g in range(groups):
             rows_r[g * GROUP + q] = part[g * span : (g + 1) * span]
 
+    left(W, w_r.at[:, pl.ds(0, n - 1)])
+    left(COTS, cots_s.at[pl.ds(0, n - 1)])
+    left(ROWS, rows_s.at[pl.ds(0, n - 3)])
+
     def order_back(g, _):
         part = rows_r[pl.ds(g * GROUP, GROUP)].reshape(GROUP * block, quarter)
         part = dot(swap[...], part).astype(BF16)
@@ -295,16 +376,44 @@
         return 0
 
     lax.fori_loop(0, groups, order_back, 0)
-    spread(BACK, lambda e: rows_s.at[e], lambda s: back_r.at[s])
+
+    def send_back(kind, first, count, sign):
+        def start(g, i):
+            at_y = lax.rem(y + i, ny)
+            pltpu.make_async_remote_copy(
+                src_ref=rows_s.at[at_y * nz + plane(-sign * (g + min(first, 1)))],
+                dst_ref=back_r.at[(first + g) * ny + y],
+                send_sem=send.at[kind],
+                recv_sem=recv.at[kind],
+                device_id=(dp, at_y * nz + plane(-sign * g)),
+                device_id_type=MESH,
+            ).start()
+            return 0
+
+        lax.fori_loop(ny, count * ny, lambda i, _: start(i // ny, i % ny), 0)
+        lax.fori_loop(1, ny, lambda i, _: start(0, i), 0)
+        pltpu.make_async_copy(
+            rows_s.at[y * nz + plane(-sign * min(first, 1))],
+            back_r.at[first * ny + y],
+            recv.at[kind],
+        ).start()
+
+    sides = ((1, far, side), (1 + far, short, -side))
+    send_back(LONG, *sides[0])
+    send_back(SHORT, *sides[1])
+    send_back(OWN, 0, 1, 0)
+    spread(M2, lambda e: m2.at[:, e], lambda s: m2_r.at[:, s])
 
     chunk = min(384, 2 * hidden)
 
-    def weight_grad(j):
-        at = pl.multiple_of(j * cols, cols)
+    def weight_grad(k):
+        at = pl.multiple_of(k * CORES * cols, CORES * cols)
 
         def rows_of(r, _):
             spot = pl.ds(pl.multiple_of(r * chunk, chunk), chunk)
-            grads[j, spot, :] = dot(pair_t[spot, :], x_mat[:, pl.ds(at, cols)]).astype(BF16)
+            part = dot(pair_t[spot, :], x_mat[:, pl.ds(at, CORES * cols)]).astype(BF16)
+            for i in range(CORES):
+                grads[k * CORES + i, spot, :] = part[:, i * cols : (i + 1) * cols]
             return 0
 
         lax.fori_loop(0, 2 * hidden // chunk, rows_of, 0)
@@ -330,10 +439,9 @@
         )
 
     for d in range(1, nx + 1):
-        weight_grad(lax.rem(x + d, nx) * CORES + 1 - core)
+        weight_grad(lax.rem(x + d, nx))
         halve(d).start()
     for d in range(1, nx + 1):
-        weight_grad(x_peer(d))
         halve(d).wait_recv()
         if d < nx:
 
@@ -345,6 +453,31 @@
 
             lax.fori_loop(0, 2 * hidden // chunk, add, 0)
             pass_on(d).start()
+
+    def sums(first, count, picks, out):
+        for q in range(QUARTERS):
+            part = back_r[first * ny : (first + count) * ny].reshape(count * ny * block, quarter)
+            out(slice(q * quarter, (q + 1) * quarter), dot(picks[q], part))
+
+    def bring(i):
+        return pltpu.make_async_remote_copy(
+            src_ref=near_tokens.at[i],
+            dst_ref=near_back.at[i],
+            send_sem=bring_send.at[i],
+            recv_sem=bring_recv.at[i],
+            device_id=(dp, y * nz + plane(-sides[i][2])),
+            device_id_type=MESH,
+        )
+
+    for i, kind in enumerate((LONG, SHORT)):
+        first, count, sign = sides[i]
+
+        def keep(spot, total, i=i):
+            near_tokens[i, :, spot] = total.astype(BF16)
+
+        arrived(kind, back_r.at[pl.ds(first * ny, count * ny)])
+        sums(first, count, picks_of[i], keep)
+        bring(i).start()
 
     for d in range(1, nx):
         pass_on(d).wait_recv()
@@ -374,14 +507,20 @@
 
     lax.fori_loop(0, groups, adam, 0)
 
-    piece = lax.broadcasted_iota(jnp.int32, (tok, n * block), 1)
-
-    arrived(BACK, back_r)
-    returned = back_r[...].reshape(n * block, quarter)
-    for q in range(QUARTERS):
-        pick = (piece == spots[0] + q * cap) | (piece == spots[1] + q * cap)
-        token_out[:, q * quarter : (q + 1) * quarter] = dot(pick.astype(BF16), returned).astype(BF16)
-
+    arrived(OWN, back_r.at[pl.ds(0, ny)])
+    for i in range(2):
+        bring(i).wait_recv()
+
+    def finish(spot, total):
+        for i in range(2):
+            total += near_back[i, :, spot].astype(F32)
+        token_out[:, spot] = total.astype(BF16)
+
+    sums(0, 1, picks_own, finish)
+
+    for i in range(2):
+        for copy in lend(i):
+            copy.wait_send()
     for d in range(1, nx):
         gather(d).wait_send()
         pass_on(d).wait_send()
@@ -390,7 +529,11 @@
         halve(d + 1).wait_send()
     left(M1, m1_r.at[:, pl.ds(0, n - 1)])
     left(M2, m2_r.at[:, pl.ds(0, n - 1)])
-    left(BACK, rows_s.at[pl.ds(0, n - 1)])
+    left(LONG, rows_s.at[pl.ds(0, far * ny - 1)])
+    left(SHORT, rows_s.at[pl.ds(0, short * ny - 1)])
+    left(OWN, rows_s.at[pl.ds(0, ny - 1)])
+    for i in range(2):
+        bring(i).wait_send()
 
 
 def place(*refs):
@@ -409,13 +552,14 @@
 ):
     ndp, n = mesh_sizes
     nx = ndp // CORES
-    nz = min(8, n)
+    nz = ALONG_Z
     ny = n // nz
     tok, width = tokens.shape
     hidden = hidden_cotangent.shape[2]
     cap = 3 * tok * 2 // (2 * n)
     per_source, cols = weights.shape[2], weights.shape[3]
     block, cot_block, slots = QUARTERS * cap, HALVES * cap, n * cap
+    plane = ny * block
     vmem = pl.BlockSpec(memory_space=pltpu.VMEM)
     hbm = pl.BlockSpec(memory_space=pl.ANY)
     shapes = [(tok, width)] + [(2, hidden, cols)] * 3
@@ -445,8 +589,18 @@
             pltpu.VMEM((nx - 1, 2 * hidden, cols), BF16),
             pltpu.VMEM((GROUP * block,) * 2, BF16),
             pltpu.VMEM((GROUP * cot_block,) * 2, BF16),
-            dma((6,)),
-            dma((6,)),
+            pltpu.VMEM((2, tok, width), BF16),
+            pltpu.VMEM((2, 2, tok), jnp.int32),
+            pltpu.VMEM((2, tok, width), BF16),
+            pltpu.VMEM((QUARTERS, tok, plane), BF16),
+            pltpu.VMEM((QUARTERS, tok, nz // 2 * plane), BF16),
+            pltpu.VMEM((QUARTERS, tok, (nz - 1 - nz // 2) * plane), BF16),
+            dma((4,)),
+            dma((4,)),
+            dma((2,)),
+            dma((2,)),
+            dma((8,)),
+            dma((8,)),
             dma((nx - 1,)),
             dma((nx - 1,)),
             dma((nx,)),
@@ -457,7 +611,7 @@
             dma((nx - 1,)),
         ],
         compiler_params=pltpu.CompilerParams(
-            collective_id=0, has_side_effects=True, vmem_limit_bytes=50 * 1024 * 1024
+            collective_id=0, has_side_effects=True, vmem_limit_bytes=53 * 1024 * 1024
         ),
         name="experts_step",
     )(

time: 210 us -> 197 us (0.938)
  Pallas kernels: 208 us -> 196 us
    pallas_call x1, Pallas kernels: 206 us -> 194 us  [per_device(): pl.pallas_call(functools.partial(kernel, nx, ny, nz, cap), out_shape=tupl...]
where the time goes in v3:
time: 197 us; the launch traced here: 196 us
  Pallas kernels  196 us (99%)
    pallas_call x1, Pallas kernels, per_device(): pl.pallas_call(functools.partial(kernel, nx, ny, nz, cap), out_shape=tupl...  194 us

profile of v3, /device:TPU:6, one launch (start us, length us, event | category | flops | bytes accessed | tf_op | source)
XLA Modules:
  0.0 196.4 jit_solution(7874335987210552005)
XLA Ops:
  0.6 193.7 %experts_step.1 = (bf16[128,3072]{1,0:T(8,128)(2,1)S(1)}, bf16[2,768,384]{2,1,0:T(8,128)(2,1)S(1)}, bf16[2,768,384]{2,1,0:T(8,128)(2,1)S(1)}, bf16[2,768,384]{2,1,0:T(8,128)(2,1)S(1)}) custom-call(s32[2,128]{1,0:T(2,128)} %bitcast.11, s32[2,128]{1,0:T(2,128)} %bitcast.12, bf16[128,3072]{1,0:T(8,128)(2,1)} %tokens.1, bf16[128,2,768]{2,1,0:T(2,128)(2,1)} %cotangent.1, ...), custom_call_target="tpu_custom_call" | custom-call | tf_op jit(solution)/shard_map/experts_step/pallas_call | solution.py:567
  194.3 2.1 %place.1 = (bf16[128,3072]{1,0:T(8,128)(2,1)}, bf16[2,768,384]{2,1,0:T(8,128)(2,1)}, bf16[2,768,384]{2,1,0:T(8,128)(2,1)}, bf16[2,768,384]{2,1,0:T(8,128)(2,1)}) custom-call(bf16[128,3072]{1,0:T(8,128)(2,1)S(1)} %get-tuple-element.12.refs_0_, bf16[2,768,384]{2,1,0:T(8,128)(2,1)S(1)} %get-tuple-element.13.refs_1_, ...), custom_call_target="tpu_custom_call" | custom-call | tf_op jit(solution)/shard_map/place/pallas_call | solution.py:626

commit v4 on v3

--- a/solution.py
+++ b/solution.py
@@ -18,11 +18,14 @@
 F32 = jnp.float32
 BF16 = jnp.bfloat16
 CORES = 2
+PIECES = 4
 QUARTERS = 4
 HALVES = 2
 ALONG_Z = 8
 GROUP = 4
-W, ROWS, COTS, M1, M2, LONG, SHORT, OWN = range(8)
+W, ROWS, COTS, LONG, SHORT, OWN, STATE = range(7)
+STATES = ((0, 0), (0, 1), (1, 0), (1, 1))
+EARLY, MIDDLE, LATE = (), (0, 1, 2), (3,)
 
 
 def dot(a, b, dims=((1,), (0,))):
@@ -46,8 +49,8 @@
     cap,
     routes,
     gates,
-    tokens,
-    cotangent,
+    tokens_hbm,
+    cotangent_hbm,
     w,
     m1,
     m2,
@@ -59,6 +62,8 @@
     rows_r,
     cots_s,
     cots_r,
+    tokens,
+    cotangent,
     scaled,
     w_r,
     m1_r,
@@ -80,6 +85,8 @@
     picks_own,
     picks_far,
     picks_short,
+    own_sum,
+    load_sem,
     near_send,
     near_recv,
     bring_send,
@@ -118,6 +125,13 @@
     def x_peer(d):
         return lax.rem(x + d, nx) * CORES + core
 
+    loads = [
+        pltpu.make_async_copy(source, landing, load_sem.at[i])
+        for i, (source, landing) in enumerate(((tokens_hbm, tokens), (cotangent_hbm, cotangent)))
+    ]
+    for load in loads:
+        load.start()
+
     barrier = pltpu.get_barrier_semaphore()
 
     def greet(i, _):
@@ -162,23 +176,28 @@
     def plane(step):
         return lax.rem(z + step + 2 * nz, nz)
 
-    def lend(i):
-        to = (dp, y * nz + plane(side * (1 - 2 * i)))
+    def lend(source, landing, kind, i):
+        return pltpu.make_async_remote_copy(
+            src_ref=source,
+            dst_ref=landing,
+            send_sem=near_send.at[2 * kind + i],
+            recv_sem=near_recv.at[2 * kind + i],
+            device_id=(dp, y * nz + plane(side * (1 - 2 * i))),
+            device_id_type=MESH,
+        )
+
+    def lent(i):
         return [
-            pltpu.make_async_remote_copy(
-                src_ref=source,
-                dst_ref=landing.at[i],
-                send_sem=near_send.at[2 * j + i],
-                recv_sem=near_recv.at[2 * j + i],
-                device_id=to,
-                device_id_type=MESH,
-            )
-            for j, (source, landing) in enumerate(((tokens, near_tokens), (routes, near_routes)))
+            lend(tokens_hbm, near_tokens.at[i], 0, i),
+            lend(routes, near_routes.at[i], 1, i),
         ]
 
+    piece_rows = tok // PIECES
     for i in range(2):
-        for copy in lend(i):
-            copy.start()
+        for j in range(PIECES):
+            rows = pl.ds(j * piece_rows, piece_rows)
+            lend(tokens_hbm.at[rows], near_tokens.at[i, rows], 0, i).start()
+        lend(routes, near_routes.at[i], 1, i).start()
     picks_of = (picks_far, picks_short)
 
     experts = n
@@ -193,6 +212,8 @@
         return rows, [jnp.sum(h * before, axis=0, keepdims=True).astype(jnp.int32) for h in hot]
 
     route_rows, pos_row = number(routes)
+    for load in loads:
+        load.wait()
 
     def column(row):
         return jnp.sum(jnp.where(earlier == later, row, jnp.zeros_like(row)), axis=1, keepdims=True)
@@ -267,6 +288,19 @@
 
     lax.fori_loop(0, groups, pack_cots, 0)
     spread(COTS, lambda e: cots_s.at[e], lambda s: cots_r.at[s])
+    moments = ((m1, m1_r), (m2, m2_r))
+
+    def spread_states(which):
+        for i in which:
+            moment, a = STATES[i]
+            source, landing = moments[moment]
+            spread(
+                STATE + i,
+                lambda e, source=source, a=a: source.at[a, e],
+                lambda s, landing=landing, a=a: landing.at[a, s],
+            )
+
+    spread_states(EARLY)
     pack_rows(0, 1, 1, (route_rows, pos_row), tokens, picks_own)
     send_rows(0, 1, 0, z)
     arrived(W, w_r)
@@ -306,11 +340,11 @@
     hand_over(0).start()
 
     for i, (first, count, sign) in enumerate(((1, far, side), (1 + far, short, -side))):
-        for copy in lend(i):
+        for copy in lent(i):
             copy.wait_recv()
         pack_rows(first, count, sign, number(near_routes.at[i]), near_tokens.at[i], picks_of[i])
         send_rows(first, count, sign, plane(-sign))
-    spread(M1, lambda e: m1.at[:, e], lambda s: m1_r.at[:, s])
+    spread_states(MIDDLE)
 
     for d in range(1, nx):
         gather(d).wait_recv()
@@ -402,7 +436,7 @@
     send_back(LONG, *sides[0])
     send_back(SHORT, *sides[1])
     send_back(OWN, 0, 1, 0)
-    spread(M2, lambda e: m2.at[:, e], lambda s: m2_r.at[:, s])
+    spread_states(LATE)
 
     chunk = min(384, 2 * hidden)
 
@@ -459,10 +493,10 @@
             part = back_r[first * ny : (first + count) * ny].reshape(count * ny * block, quarter)
             out(slice(q * quarter, (q + 1) * quarter), dot(picks[q], part))
 
-    def bring(i):
+    def bring(i, spot=slice(None)):
         return pltpu.make_async_remote_copy(
-            src_ref=near_tokens.at[i],
-            dst_ref=near_back.at[i],
+            src_ref=near_tokens.at[i, :, spot],
+            dst_ref=near_back.at[i, :, spot],
             send_sem=bring_send.at[i],
             recv_sem=bring_recv.at[i],
             device_id=(dp, y * nz + plane(-sides[i][2])),
@@ -474,15 +508,21 @@
 
         def keep(spot, total, i=i):
             near_tokens[i, :, spot] = total.astype(BF16)
+            bring(i, pl.ds(spot.start, quarter)).start()
 
         arrived(kind, back_r.at[pl.ds(first * ny, count * ny)])
         sums(first, count, picks_of[i], keep)
-        bring(i).start()
+
+    def keep_own(spot, total):
+        own_sum[:, spot] = total
+
+    arrived(OWN, back_r.at[pl.ds(0, ny)])
+    sums(0, 1, picks_own, keep_own)
 
     for d in range(1, nx):
         pass_on(d).wait_recv()
-    arrived(M1, m1_r)
-    arrived(M2, m2_r)
+    for i, (moment, a) in enumerate(STATES):
+        arrived(STATE + i, moments[moment][1].at[a])
 
     rows = GROUP * per_source
 
@@ -507,19 +547,12 @@
 
     lax.fori_loop(0, groups, adam, 0)
 
-    arrived(OWN, back_r.at[pl.ds(0, ny)])
     for i in range(2):
         bring(i).wait_recv()
-
-    def finish(spot, total):
-        for i in range(2):
-            total += near_back[i, :, spot].astype(F32)
-        token_out[:, spot] = total.astype(BF16)
-
-    sums(0, 1, picks_own, finish)
+    token_out[...] = (own_sum[...] + near_back[0].astype(F32) + near_back[1].astype(F32)).astype(BF16)
 
     for i in range(2):
-        for copy in lend(i):
+        for copy in lent(i):
             copy.wait_send()
     for d in range(1, nx):
         gather(d).wait_send()
@@ -527,8 +560,8 @@
     for d in range(nx):
         hand_over(d).wait_send()
         halve(d + 1).wait_send()
-    left(M1, m1_r.at[:, pl.ds(0, n - 1)])
-    left(M2, m2_r.at[:, pl.ds(0, n - 1)])
+    for i, (moment, a) in enumerate(STATES):
+        left(STATE + i, moments[moment][1].at[a, pl.ds(0, n - 1)])
     left(LONG, rows_s.at[pl.ds(0, far * ny - 1)])
     left(SHORT, rows_s.at[pl.ds(0, short * ny - 1)])
     left(OWN, rows_s.at[pl.ds(0, ny - 1)])
@@ -538,9 +571,14 @@
 
 def place(*refs):
     count = (len(refs) - 1) // 2
-    copies = [
-        pltpu.make_async_copy(refs[i], refs[count + i], refs[-1].at[i]) for i in range(count)
-    ]
+    copies = []
+    for i in range(count):
+        half = refs[i].shape[0] // 2
+        for j in range(2):
+            part = pl.ds(j * half, half)
+            copies.append(
+                pltpu.make_async_copy(refs[i].at[part], refs[count + i].at[part], refs[-1].at[2 * i + j])
+            )
     for copy in copies:
         copy.start()
     for copy in copies:
@@ -567,13 +605,15 @@
     results = pl.pallas_call(
         functools.partial(kernel, nx, ny, nz, cap),
         out_shape=tuple(pltpu.VMEM(shape, BF16) for shape in shapes),
-        in_specs=[vmem] * 4 + [hbm] * 3,
+        in_specs=[vmem] * 2 + [hbm] * 5,
         out_specs=(vmem,) * 4,
         scratch_shapes=[
             pltpu.VMEM((n, block, width // QUARTERS), BF16),
             pltpu.VMEM((n, block, width // QUARTERS), BF16),
             pltpu.VMEM((n, cot_block, hidden // HALVES), BF16),
             pltpu.VMEM((n, cot_block, hidden // HALVES), BF16),
+            pltpu.VMEM((tok, width), BF16),
+            pltpu.VMEM((tok, 2, hidden), BF16),
             pltpu.VMEM((tok, 2 * hidden), BF16),
             pltpu.VMEM((2, n, per_source, cols), BF16),
             pltpu.VMEM((2, n, per_source, cols), BF16),
@@ -595,12 +635,14 @@
             pltpu.VMEM((QUARTERS, tok, plane), BF16),
             pltpu.VMEM((QUARTERS, tok, nz // 2 * plane), BF16),
             pltpu.VMEM((QUARTERS, tok, (nz - 1 - nz // 2) * plane), BF16),
+            pltpu.VMEM((tok, width), F32),
+            dma((2,)),
             dma((4,)),
             dma((4,)),
             dma((2,)),
             dma((2,)),
-            dma((8,)),
-            dma((8,)),
+            dma((STATE + len(STATES),)),
+            dma((STATE + len(STATES),)),
             dma((nx - 1,)),
             dma((nx - 1,)),
             dma((nx,)),
@@ -628,7 +670,7 @@
         out_shape=tuple(jax.ShapeDtypeStruct(shape, BF16) for shape in shapes),
         in_specs=[vmem] * 4,
         out_specs=(hbm,) * 4,
-        scratch_shapes=[dma((4,))],
+        scratch_shapes=[dma((8,))],
         compiler_params=pltpu.CompilerParams(vmem_limit_bytes=1024 * 1024),
         name="place",
     )(*(pltpu.with_memory_space_constraint(result, pltpu.VMEM) for result in results))

time: 197 us -> 196 us (level)
  no operation moved by 1% of the time
where the time goes in v4:
time: 196 us
  Pallas kernels  195 us (99%)
    pallas_call x1, Pallas kernels, per_device(): pl.pallas_call(functools.partial(kernel, nx, ny, nz, cap), out_shape=tupl...  193 us

profile of v4, /device:TPU:6, one launch (start us, length us, event | category | flops | bytes accessed | tf_op | source)
XLA Modules:
  0.0 195.9 jit_solution(5364827210902833430)
XLA Ops:
  0.6 193.0 %experts_step.1 = (bf16[128,3072]{1,0:T(8,128)(2,1)S(1)}, bf16[2,768,384]{2,1,0:T(8,128)(2,1)S(1)}, bf16[2,768,384]{2,1,0:T(8,128)(2,1)S(1)}, bf16[2,768,384]{2,1,0:T(8,128)(2,1)S(1)}) custom-call(s32[2,128]{1,0:T(2,128)} %bitcast.11, s32[2,128]{1,0:T(2,128)} %bitcast.12, bf16[128,3072]{1,0:T(8,128)(2,1)} %tokens_hbm.1, bf16[128,2,768]{2,1,0:T(2,128)(2,1)} %cotangent_hbm.1, ...), custom_call_target="tpu_custom_call" | custom-call | tf_op jit(solution)/shard_map/experts_step/pallas_call | solution.py:605
  193.6 2.1 %place.1 = (bf16[128,3072]{1,0:T(8,128)(2,1)}, bf16[2,768,384]{2,1,0:T(8,128)(2,1)}, bf16[2,768,384]{2,1,0:T(8,128)(2,1)}, bf16[2,768,384]{2,1,0:T(8,128)(2,1)}) custom-call(bf16[128,3072]{1,0:T(8,128)(2,1)S(1)} %get-tuple-element.12.refs_0_, bf16[2,768,384]{2,1,0:T(8,128)(2,1)S(1)} %get-tuple-element.13.refs_1_, ...), custom_call_target="tpu_custom_call" | custom-call | tf_op jit(solution)/shard_map/place/pallas_call | solution.py:668

commit v5 on v4

--- a/solution.py
+++ b/solution.py
@@ -493,12 +493,13 @@
             part = back_r[first * ny : (first + count) * ny].reshape(count * ny * block, quarter)
             out(slice(q * quarter, (q + 1) * quarter), dot(picks[q], part))
 
-    def bring(i, spot=slice(None)):
+    def bring(i, q):
+        spot = pl.ds(q * quarter, quarter)
         return pltpu.make_async_remote_copy(
             src_ref=near_tokens.at[i, :, spot],
             dst_ref=near_back.at[i, :, spot],
-            send_sem=bring_send.at[i],
-            recv_sem=bring_recv.at[i],
+            send_sem=bring_send.at[i, q],
+            recv_sem=bring_recv.at[i, q],
             device_id=(dp, y * nz + plane(-sides[i][2])),
             device_id_type=MESH,
         )
@@ -508,7 +509,7 @@
 
         def keep(spot, total, i=i):
             near_tokens[i, :, spot] = total.astype(BF16)
-            bring(i, pl.ds(spot.start, quarter)).start()
+            bring(i, spot.start // quarter).start()
 
         arrived(kind, back_r.at[pl.ds(first * ny, count * ny)])
         sums(first, count, picks_of[i], keep)
@@ -547,9 +548,13 @@
 
     lax.fori_loop(0, groups, adam, 0)
 
-    for i in range(2):
-        bring(i).wait_recv()
-    token_out[...] = (own_sum[...] + near_back[0].astype(F32) + near_back[1].astype(F32)).astype(BF16)
+    for q in range(QUARTERS):
+        spot = slice(q * quarter, (q + 1) * quarter)
+        total = own_sum[:, spot]
+        for i in range(2):
+            bring(i, q).wait_recv()
+            total += near_back[i, :, spot].astype(F32)
+        token_out[:, spot] = total.astype(BF16)
 
     for i in range(2):
         for copy in lent(i):
@@ -566,7 +571,8 @@
     left(SHORT, rows_s.at[pl.ds(0, short * ny - 1)])
     left(OWN, rows_s.at[pl.ds(0, ny - 1)])
     for i in range(2):
-        bring(i).wait_send()
+        for q in range(QUARTERS):
+            bring(i, q).wait_send()
 
 
 def place(*refs):
@@ -639,8 +645,8 @@
             dma((2,)),
             dma((4,)),
             dma((4,)),
-            dma((2,)),
-            dma((2,)),
+            dma((2, QUARTERS)),
+            dma((2, QUARTERS)),
             dma((STATE + len(STATES),)),
             dma((STATE + len(STATES),)),
             dma((nx - 1,)),

time: 196 us -> 196 us (level)
  no operation moved by 1% of the time
where the time goes in v5:
time: 196 us
  Pallas kernels  195 us (99%)
    pallas_call x1, Pallas kernels, per_device(): pl.pallas_call(functools.partial(kernel, nx, ny, nz, cap), out_shape=tupl...  193 us

profile of v5, /device:TPU:6, one launch (start us, length us, event | category | flops | bytes accessed | tf_op | source)
XLA Modules:
  0.0 195.9 jit_solution(944942489480520536)
XLA Ops:
  0.6 192.9 %experts_step.1 = (bf16[128,3072]{1,0:T(8,128)(2,1)S(1)}, bf16[2,768,384]{2,1,0:T(8,128)(2,1)S(1)}, bf16[2,768,384]{2,1,0:T(8,128)(2,1)S(1)}, bf16[2,768,384]{2,1,0:T(8,128)(2,1)S(1)}) custom-call(s32[2,128]{1,0:T(2,128)} %bitcast.11, s32[2,128]{1,0:T(2,128)} %bitcast.12, bf16[128,3072]{1,0:T(8,128)(2,1)} %tokens_hbm.1, bf16[128,2,768]{2,1,0:T(2,128)(2,1)} %cotangent_hbm.1, ...), custom_call_target="tpu_custom_call" | custom-call | tf_op jit(solution)/shard_map/experts_step/pallas_call | solution.py:611
  193.6 2.1 %place.1 = (bf16[128,3072]{1,0:T(8,128)(2,1)}, bf16[2,768,384]{2,1,0:T(8,128)(2,1)}, bf16[2,768,384]{2,1,0:T(8,128)(2,1)}, bf16[2,768,384]{2,1,0:T(8,128)(2,1)}) custom-call(bf16[128,3072]{1,0:T(8,128)(2,1)S(1)} %get-tuple-element.12.refs_0_, bf16[2,768,384]{2,1,0:T(8,128)(2,1)S(1)} %get-tuple-element.13.refs_1_, ...), custom_call_target="tpu_custom_call" | custom-call | tf_op jit(solution)/shard_map/place/pallas_call | solution.py:674
